TPU v7x, 256 devices: a whole 4x4x8 slice. The times are simulated.
256 devices in a mesh: dp: 16 (over x, y), cent: 16 (over z, core).
Axes of the slice: x: 4, y: 4, z: 8, core: 2. Of those that a mesh axis runs over, the one named last changes fastest.
Arguments:
- embeddings: bfloat16 [32768, 1024], P('dp')
- centroids: bfloat16 [8192, 1024], P('cent')
- col_start: float32 [8192], P('cent'), may hold values from -6 to 6
Outputs:
- new_centroids: bfloat16 [8192, 1024], P('cent')
- row_potential: float32 [32768], P('dp')
- col_potential: float32 [8192], P('cent')
All inputs are finite; a program needn't handle non-finite values.
Results may differ from a plain program's by a relative error of at most 0.0048.
Values may be sent and summed in bfloat16 or wider, within the bound.
A program may use at most 64 MiB of HBM per device.

v0:
```python
import math

import jax
import jax.numpy as jnp
from jax import lax
from jax.sharding import PartitionSpec as P

ITERS = 3


def merged(x, axis, combine):
    everything = jax.tree.map(lambda part: lax.all_gather(part, axis), x)
    leading = jax.tree.map(lambda part: part[0], everything)

    def hop(k, so_far):
        return combine(so_far, jax.tree.map(lambda part: part[k], everything))

    return lax.fori_loop(1, lax.axis_size(axis), hop, leading)


def join_totals(first, second):
    joined = jnp.maximum(first[0], second[0])
    total = first[1] * jnp.exp(first[0] - joined) + second[1] * jnp.exp(second[0] - joined)
    return (joined, total)


def on_device(embeddings, centroids, col_start):
    rows_here = embeddings.shape[0]
    cent_here = centroids.shape[0]
    n_total = float(rows_here * lax.axis_size("dp"))
    k_total = float(cent_here * lax.axis_size("cent"))
    factor = 1.0 / math.sqrt(embeddings.shape[1])
    col_now = col_start
    row_now = jnp.zeros((rows_here,), jnp.float32)
    scores = None
    for step_index in range(ITERS):
        product = lax.dot_general(
            embeddings, centroids, (((1,), (1,)), ((), ())), preferred_element_type=jnp.float32
        )
        scores = product * factor
        shifted = scores + col_now[None, :]
        local_peak = jnp.max(shifted, axis=1)
        peak = lax.pmax(local_peak, "cent")
        mass = lax.psum(jnp.sum(jnp.exp(shifted - peak[:, None]), axis=1), "cent")
        row_now = -jnp.log(n_total) - (peak + jnp.log(mass))
        lifted = scores + row_now[:, None]
        block_peak = jnp.max(lifted, axis=0)
        block_mass = jnp.sum(jnp.exp(lifted - block_peak[None, :]), axis=0)
        col_peak, col_mass = merged((block_peak, block_mass), "dp", join_totals)
        col_now = -jnp.log(k_total) - (col_peak + jnp.log(col_mass))
    plan = jnp.exp(scores + row_now[:, None] + col_now[None, :]).astype(jnp.bfloat16)
    partial_sums = lax.dot_general(
        plan, embeddings, (((0,), (0,)), ((), ())), preferred_element_type=jnp.float32
    )
    whole = lax.psum(partial_sums, "dp")
    new_centroids = (whole * k_total).astype(jnp.bfloat16)
    return (new_centroids, row_now, col_now)


def solution(mesh):
    placed = (P("dp", None), P("cent", None), P("cent"))
    return jax.shard_map(
        on_device,
        mesh=mesh,
        in_specs=placed,
        out_specs=(P("cent", None), P("dp"), P("cent")),
        check_vma=False,
    )
```

profile of v0, /device:TPU:1, one launch (start us, length us, event | category | flops | bytes accessed | tf_op | source)
XLA Modules:
  0.0 440.7 jit_solution(8117496304807389955)
XLA Ops:
  7.2 0.0 copy-start
  7.2 0.0 all-reduce.2.cloned.1.call-start
  7.2 1.2 copy-done
  8.4 0.0 copy-start.5
  8.4 6.6 %add_reduce_fusion.4 = (f32[2048]{0:T(1024)S(1)}, f32[2048,512]{1,0:T(8,128)}) fusion(f32[512]{0:T(512)} %param.11, bf16[2048,1024]{1,0:T(8,128)(2,1)} %param.9, bf16[512,1024]{1,0:T(8,128)(2,1)S(1)} %copy-done), kind=kOutput, calls=%fused_computation.20 | convolution fusion | flops 2150627328 | bytes 9447424 | tf_op jit(solution)/shard_map/dot_general | solution.py:37
  15.0 27.9 %pmax.21 = f32[2048]{0:T(1024)S(1)} all-reduce(f32[2048]{0:T(1024)S(1)} %get-tuple-element.450), channel_id=1, replica_groups=mesh['dp'=16,'cent'=16] {'cent'}, use_global_device_ids=true, to_apply=%region_1.0 | all-reduce | flops 2048 | bytes 16384 | tf_op jit(solution)/shard_map/pmax | solution.py:43
  42.9 0.0 copy-done.5
  42.9 3.2 exponential_reduce_fusion.5
  46.1 26.3 %psum.28 = f32[2048]{0:T(1024)S(1)} all-reduce(f32[2048]{0:T(1024)S(1)} %exponential_reduce_fusion.5), channel_id=1, replica_groups=mesh['dp'=16,'cent'=16] {'cent'}, use_global_device_ids=true, to_apply=%region_3.0 | all-reduce | flops 2048 | bytes 16384 | tf_op jit(solution)/shard_map/psum | solution.py:44
  72.4 0.0 copy-start.1
  72.4 2.7 add_reduce_fusion.3
  75.1 0.7 copy-done.1
  75.8 0.8 exponential_reduce_fusion.4
  76.6 18.1 %all-gather.6 = f32[16,1,512]{2,1,0:T(1,128)S(1)} all-gather(f32[1,1,512]{2,1,0:T(1,128)S(1)} %bitcast.70), channel_id=2, replica_groups=mesh['dp'=16,'cent'=16] {'dp'}, dimensions={0}, use_global_device_ids=true | all-gather | bytes 34816 | tf_op jit(solution)/shard_map/all_gather | solution.py:12
  94.7 17.3 %all-gather.7 = f32[16,1,512]{2,1,0:T(1,128)S(1)} all-gather(f32[1,1,512]{2,1,0:T(1,128)S(1)} %bitcast.72), channel_id=3, replica_groups=mesh['dp'=16,'cent'=16] {'dp'}, dimensions={0}, use_global_device_ids=true | all-gather | bytes 34816 | tf_op jit(solution)/shard_map/all_gather | solution.py:12
  112.0 0.9 while.51
  112.9 2.5 add_reduce_fusion.2
  115.5 34.9 %pmax.22 = f32[2048]{0:T(1024)S(1)} all-reduce(f32[2048]{0:T(1024)S(1)} %add_reduce_fusion.2), channel_id=1, replica_groups=mesh['dp'=16,'cent'=16] {'cent'}, use_global_device_ids=true, to_apply=%region_9.0 | all-reduce | flops 2048 | bytes 16384 | tf_op jit(solution)/shard_map/pmax | solution.py:43
  150.4 3.2 exponential_reduce_fusion.3
  153.6 24.1 %psum.29 = f32[2048]{0:T(1024)S(1)} all-reduce(f32[2048]{0:T(1024)S(1)} %exponential_reduce_fusion.3), channel_id=1, replica_groups=mesh['dp'=16,'cent'=16] {'cent'}, use_global_device_ids=true, to_apply=%region_11.0 | all-reduce | flops 2048 | bytes 16384 | tf_op jit(solution)/shard_map/psum | solution.py:44
  177.6 0.0 copy-start.2
  177.7 2.7 add_reduce_fusion.1
  180.3 0.7 copy-done.2
  181.1 0.8 exponential_reduce_fusion.2
  181.8 15.6 %all-gather.8 = f32[16,1,512]{2,1,0:T(1,128)S(1)} all-gather(f32[1,1,512]{2,1,0:T(1,128)S(1)} %bitcast.71), channel_id=4, replica_groups=mesh['dp'=16,'cent'=16] {'dp'}, dimensions={0}, use_global_device_ids=true | all-gather | bytes 34816 | tf_op jit(solution)/shard_map/all_gather | solution.py:12
  197.4 17.3 %all-gather.9 = f32[16,1,512]{2,1,0:T(1,128)S(1)} all-gather(f32[1,1,512]{2,1,0:T(1,128)S(1)} %bitcast.73), channel_id=5, replica_groups=mesh['dp'=16,'cent'=16] {'dp'}, dimensions={0}, use_global_device_ids=true | all-gather | bytes 34816 | tf_op jit(solution)/shard_map/all_gather | solution.py:12
  214.7 0.9 while.52
  215.6 2.5 add_reduce_fusion
  218.2 34.9 %pmax.23 = f32[2048]{0:T(1024)S(1)} all-reduce(f32[2048]{0:T(1024)S(1)} %add_reduce_fusion), channel_id=1, replica_groups=mesh['dp'=16,'cent'=16] {'cent'}, use_global_device_ids=true, to_apply=%region_17.0 | all-reduce | flops 2048 | bytes 16384 | tf_op jit(solution)/shard_map/pmax | solution.py:43
  253.1 3.2 exponential_reduce_fusion.1
  256.3 24.1 %psum.30 = f32[2048]{0:T(1024)S(1)} all-reduce(f32[2048]{0:T(1024)S(1)} %exponential_reduce_fusion.1), channel_id=1, replica_groups=mesh['dp'=16,'cent'=16] {'cent'}, use_global_device_ids=true, to_apply=%region_19.0 | all-reduce | flops 2048 | bytes 16384 | tf_op jit(solution)/shard_map/psum | solution.py:44
  280.3 0.0 copy-start.3
  280.4 0.0 copy-start.4
  280.4 2.7 add_reduce_fusion.5
  283.1 0.7 copy-done.3
  283.8 0.8 exponential_reduce_fusion
  284.6 15.6 %all-gather.11 = f32[16,1,512]{2,1,0:T(1,128)S(1)} all-gather(f32[1,1,512]{2,1,0:T(1,128)S(1)} %bitcast.74), channel_id=7, replica_groups=mesh['dp'=16,'cent'=16] {'dp'}, dimensions={0}, use_global_device_ids=true | all-gather | bytes 34816 | tf_op jit(solution)/shard_map/all_gather | solution.py:12
  300.1 17.5 %all-gather.10 = f32[16,1,512]{2,1,0:T(1,128)S(1)} all-gather(f32[1,1,512]{2,1,0:T(1,128)S(1)} %bitcast.69), channel_id=6, replica_groups=mesh['dp'=16,'cent'=16] {'dp'}, dimensions={0}, use_global_device_ids=true | all-gather | bytes 34816 | tf_op jit(solution)/shard_map/all_gather | solution.py:12
  317.6 0.9 while.53
  318.5 0.0 copy-done.4
  318.5 0.0 copy-start.6
  318.5 7.3 %fusion = f32[512,1024]{1,0:T(8,128)} fusion(bf16[2048,1024]{1,0:T(8,128)(2,1)} %param.9, f32[2048,512]{1,0:T(8,128)} %get-tuple-element.451, f32[512]{0:T(512)S(1)} %add_subtract_fusion.3, f32[2048]{0:T(1024)S(1)} %add_subtract_fusion), kind=kOutput, calls=%fused_computation.23 | convolution fusion | flops 2150629376 | bytes 10496000 | tf_op jit(solution)/shard_map/dot_general | solution.py:52
  325.8 0.0 copy-done.6
  325.8 0.0 all-reduce.2.cloned.1.call-update
  325.8 105.3 %all-reduce.2.cloned.1.call-done = f32[512,1024]{1,0:T(8,128)} async-done(((f32[512,1024]{1,0:T(8,128)}), f32[512,1024]{1,0:T(8,128)}) %all-reduce.2.cloned.1.call-update) | async-done | bytes 2097168 | tf_op jit(solution)/shard_map/psum | solution.py:55
  431.1 2.8 multiply_convert_fusion
  (108 shorter events, 1.6 us)
Async XLA Ops:
  7.2 1.2 copy-start
  7.2 423.9 %all-reduce.2.cloned.1.call-start = ((), (), s32[]{:S(2)}) async-start(), calls=%async_computation | async-start | bytes 4194304 | tf_op jit(solution)/shard_map/psum | solution.py:55
  8.4 34.5 %copy-start.5 = (f32[512]{0:T(512)S(1)}, f32[512]{0:T(512)}, u32[]{:S(2)}) copy-start(f32[512]{0:T(512)} %param.11) | copy-start | bytes 6148
  72.4 3.5 copy-start.1
  177.6 3.5 copy-start.2
  280.3 3.5 copy-start.3
  280.4 38.2 %copy-start.4 = (f32[2048]{0:T(1024)}, f32[2048]{0:T(1024)S(1)}, u32[]{:S(2)}) copy-start(f32[2048]{0:T(1024)S(1)} %add_subtract_fusion) | copy-start | bytes 24580
  318.5 7.3 %copy-start.6 = (f32[512]{0:T(512)}, f32[512]{0:T(512)S(1)}, u32[]{:S(2)}) copy-start(f32[512]{0:T(512)S(1)} %add_subtract_fusion.3) | copy-start | bytes 6148
Sparse Core Ops, SparseCore 0:
  325.9 105.0 all-reduce.1
where the time goes:
time: 441 us
  blocking collectives  273 us (62%)
  waiting for transfers between devices  105 us (24%)
  other arithmetic  28.8 us (7%)
  between operations  14.3 us (3%)
  matrix products  13.8 us (3%)
    psum x1, waiting for transfers between devices, on_device(): whole = lax.psum(partial_sums, 'dp')  105 us
    all_gather x6, blocking collectives, merged(): everything = jax.tree.map(lambda part: lax.all_gather(part, axis), x)  101 us
    pmax x3, blocking collectives, on_device(): peak = lax.pmax(local_peak, 'cent')  97.7 us
    psum x3, blocking collectives, on_device(): mass = lax.psum(jnp.sum(jnp.exp(shifted - peak[:, None]), axis=1), 'cent')  74.4 us
    reduce_sum x3, other arithmetic, on_device(): mass = lax.psum(jnp.sum(jnp.exp(shifted - peak[:, None]), axis=1), 'cent')  9.55 us
  transfers between devices with their start and end apart: 1, of which 1 were waited for; matrix products, arithmetic and copies ran while one was open for 0% of the time, Pallas kernels for 0%

commit v1 on v0

v1 whole, which is shorter than its diff:
```python
import functools
import math

import jax
import jax.numpy as jnp
from jax import lax
from jax.experimental import pallas as pl
from jax.experimental.pallas import tpu as pltpu
from jax.sharding import PartitionSpec as P

MESH = pl.DeviceIdType.MESH
LOG2E = math.log2(math.e)
LN2 = math.log(2.0)
L = 128
BLK = 256
SUB = 32


def diag_mask():
    return lax.broadcasted_iota(jnp.int32, (L, L), 0) == lax.broadcasted_iota(jnp.int32, (L, L), 1)


def to_column(row):
    spread = jnp.where(diag_mask(), jnp.broadcast_to(row, (L, L)), 0.0)
    return jnp.broadcast_to(jnp.sum(spread, axis=1, keepdims=True), (L, L))


def to_row(column):
    return jnp.sum(jnp.where(diag_mask(), column, 0.0), axis=0, keepdims=True)


def kernel(
    nd, nc, side, n_total, k_total,
    g_ref, c_hbm, e_hbm,
    out_hbm, rp_ref, cp_ref,
    cv, ev, tm, am, bm, gcol, col1, col2, rrow, crow,
    l_all, rho2, rho3, lc_all, cs2, cs3,
    p1s, p1r, p2s, p2r, p3s,
    load_sem, barrier_unused, rs_sem, rr_sem, cs_sem, cr_sem,
    b1s_sem, b1r_sem, b2s_sem, b2r_sem, b3s_sem, b3r_sem, own_sem,
):
    kc, d = cv.shape
    nk = tm.shape[0]
    nb = nk * L // BLK
    nj = kc // L
    dp = lax.axis_index("dp")
    ce = lax.axis_index("cent")
    x, y = dp // side, lax.rem(dp, side)

    barrier = pltpu.get_barrier_semaphore()

    def greet_cent(k, c):
        pl.semaphore_signal(barrier, inc=1, device_id=(dp, lax.rem(ce + k, nc)), device_id_type=MESH)
        return c

    def greet_dp(k, c):
        pl.semaphore_signal(barrier, inc=1, device_id=(lax.rem(dp + k, nd), ce), device_id_type=MESH)
        return c

    lax.fori_loop(1, nc, greet_cent, 0)
    lax.fori_loop(1, nd, greet_dp, 0)

    c_load = pltpu.make_async_copy(c_hbm, cv, load_sem.at[nb])
    c_load.start()

    def e_load(b):
        rows = pl.ds(b * BLK, BLK)
        return pltpu.make_async_copy(e_hbm.at[rows], ev.at[rows], load_sem.at[b])

    for b in range(nb):
        e_load(b).start()

    for t in range(nj):
        gcol[pl.ds(t * L, L), :] = to_column(g_ref[pl.ds(t, 1), :] * LOG2E)
    c_load.wait()

    scale = LOG2E / math.sqrt(d)

    def score_block(b, carry):
        e_load(b).wait()
        block = ev[pl.ds(pl.multiple_of(b * BLK, BLK), BLK), :]
        product = lax.dot_general(cv[...], block, (((1,), (1,)), ((), ())), preferred_element_type=jnp.float32)
        product = product * scale
        for h in range(BLK // L):
            tm[b * (BLK // L) + h] = product[:, h * L : (h + 1) * L]
        for h in range(BLK // L):
            k = b * (BLK // L) + h
            peak = jnp.max(tm[k] + gcol[...], axis=0, keepdims=True)
            mass = jnp.sum(jnp.exp2(tm[k] + gcol[...] - peak), axis=0, keepdims=True)
            l_all[ce, pl.ds(k, 1), :] = peak + jnp.log2(mass)
        return carry

    lax.fori_loop(0, nb, score_block, 0)
    pl.semaphore_wait(barrier, nc - 1 + nd - 1)

    def cent_copy(phase, buf, k):
        to = lax.rem(ce + k, nc)
        return pltpu.make_async_remote_copy(
            src_ref=buf.at[ce], dst_ref=buf.at[ce],
            send_sem=rs_sem.at[phase, to], recv_sem=rr_sem.at[phase, ce],
            device_id=(dp, to), device_id_type=MESH,
        )

    def cent_arrival(phase, buf, k):
        fr = lax.rem(ce + k, nc)
        return pltpu.make_async_remote_copy(
            src_ref=buf.at[fr], dst_ref=buf.at[fr],
            send_sem=rs_sem.at[phase, fr], recv_sem=rr_sem.at[phase, fr],
            device_id=(dp, fr), device_id_type=MESH,
        )

    def dp_copy(phase, buf, k):
        to = lax.rem(dp + k, nd)
        return pltpu.make_async_remote_copy(
            src_ref=buf.at[dp], dst_ref=buf.at[dp],
            send_sem=cs_sem.at[phase, to], recv_sem=cr_sem.at[phase, dp],
            device_id=(to, ce), device_id_type=MESH,
        )

    def dp_arrival(phase, buf, k):
        fr = lax.rem(dp + k, nd)
        return pltpu.make_async_remote_copy(
            src_ref=buf.at[fr], dst_ref=buf.at[fr],
            send_sem=cs_sem.at[phase, fr], recv_sem=cr_sem.at[phase, fr],
            device_id=(fr, ce), device_id_type=MESH,
        )

    def loop(n, act):
        def step(k, c):
            act(k)
            return c

        lax.fori_loop(1, n, step, 0)

    def cent_exchange(phase, buf):
        loop(nc, lambda k: cent_copy(phase, buf, k).start())
        loop(nc, lambda k: cent_arrival(phase, buf, k).wait_recv())

    def dp_start(phase, buf):
        loop(nd, lambda k: dp_copy(phase, buf, k).start())

    def dp_finish(phase, buf):
        loop(nd, lambda k: dp_arrival(phase, buf, k).wait_recv())

    def joined(buf, n):
        peak = buf[0]
        for s in range(1, n):
            peak = jnp.maximum(peak, buf[s])
        total = jnp.exp2(buf[0] - peak)
        for s in range(1, n):
            total = total + jnp.exp2(buf[s] - peak)
        return peak + jnp.log2(total)

    def added(buf, n):
        total = buf[0].astype(jnp.float32)
        for s in range(1, n):
            total = total + buf[s].astype(jnp.float32)
        return total

    cent_exchange(0, l_all)
    rrow[...] = -math.log2(n_total) - joined(l_all, nc)

    def first_columns(jb, carry):
        rows = pl.ds(pl.multiple_of(jb * SUB, SUB), SUB)
        peak = tm[0, rows, :] + rrow[pl.ds(0, 1), :]
        for k in range(1, nk):
            peak = jnp.maximum(peak, tm[k, rows, :] + rrow[pl.ds(k, 1), :])
        peak = jnp.broadcast_to(jnp.max(peak, axis=1, keepdims=True), (SUB, L))
        mass = jnp.zeros((SUB, L), jnp.float32)
        for k in range(nk):
            value = jnp.exp2(tm[k, rows, :] + rrow[pl.ds(k, 1), :] - peak)
            am[k, rows, :] = value
            mass = mass + value
        col1[rows, :] = peak
        col2[rows, :] = jnp.broadcast_to(jnp.sum(mass, axis=1, keepdims=True), (SUB, L))
        return carry

    lax.fori_loop(0, kc // SUB, first_columns, 0)
    for t in range(nj):
        top = to_row(col1[pl.ds(t * L, L), :])
        crow[pl.ds(t, 1), :] = top
        lc_all[dp, pl.ds(t, 1), :] = top + jnp.log2(to_row(col2[pl.ds(t * L, L), :]))
    dp_start(0, lc_all)
    dp_finish(0, lc_all)
    g_one = -math.log2(k_total) - joined(lc_all, nd)
    lift = jnp.exp2(crow[...] + g_one)
    crow[...] = g_one
    for t in range(nj):
        col1[pl.ds(t * L, L), :] = to_column(lift[t : t + 1, :])

    def second_rows(k, carry):
        value = am[k] * col1[...]
        am[k] = value
        rho2[ce, pl.ds(k, 1), :] = jnp.sum(value, axis=0, keepdims=True)
        return carry

    lax.fori_loop(0, nk, second_rows, 0)
    cent_exchange(1, rho2)
    u_two = 1.0 / (n_total * added(rho2, nc))
    bm_rows = rrow

    def column_sums(u, target, keep):
        def body(jb, carry):
            rows = pl.ds(pl.multiple_of(jb * SUB, SUB), SUB)
            mass = jnp.zeros((SUB, L), jnp.float32)
            for k in range(nk):
                value = am[k, rows, :] * u[k : k + 1, :]
                if keep:
                    bm[rows, k * L : (k + 1) * L] = value.astype(jnp.bfloat16)
                mass = mass + value
            col2[rows, :] = jnp.broadcast_to(jnp.sum(mass, axis=1, keepdims=True), (SUB, L))
            return carry

        lax.fori_loop(0, kc // SUB, body, 0)
        for t in range(nj):
            target[dp, pl.ds(t, 1), :] = to_row(col2[pl.ds(t * L, L), :])

    column_sums(u_two, cs2, False)
    dp_start(1, cs2)
    dp_finish(1, cs2)
    v_two = 1.0 / (k_total * added(cs2, nd))
    for t in range(nj):
        col1[pl.ds(t * L, L), :] = to_column(v_two[t : t + 1, :])

    def third_rows(k, carry):
        rho3[ce, pl.ds(k, 1), :] = jnp.sum(am[k] * col1[...], axis=0, keepdims=True)
        return carry

    lax.fori_loop(0, nk, third_rows, 0)
    cent_exchange(2, rho3)
    u_three = 1.0 / (n_total * added(rho3, nc))
    rp_ref[...] = (bm_rows[...] + jnp.log2(u_three)) * LN2

    column_sums(u_three, cs3, True)
    dp_start(2, cs3)

    hr = kc // 2
    dq = d // side
    here = (x, y)

    def along(h, stage, i):
        if (h + stage) % 2 == 0:
            return (i * side + y, ce)
        return (x * side + i, ce)

    def place(h, stage):
        return here[(h + stage) % 2]

    def b1_copy(h, i):
        me = place(h, 0)
        return pltpu.make_async_remote_copy(
            src_ref=p1s.at[h, i], dst_ref=p1r.at[h, me],
            send_sem=b1s_sem.at[h, i], recv_sem=b1r_sem.at[h, me],
            device_id=along(h, 0, i), device_id_type=MESH,
        )

    def b1_arrival(h, i):
        return pltpu.make_async_remote_copy(
            src_ref=p1s.at[h, i], dst_ref=p1r.at[h, i],
            send_sem=b1s_sem.at[h, i], recv_sem=b1r_sem.at[h, i],
            device_id=along(h, 0, i), device_id_type=MESH,
        )

    def b2_copy(h, i):
        me = place(h, 1)
        return pltpu.make_async_remote_copy(
            src_ref=p2r.at[h, me], dst_ref=p2r.at[h, me],
            send_sem=b2s_sem.at[h, i], recv_sem=b2r_sem.at[h, me],
            device_id=along(h, 1, i), device_id_type=MESH,
        )

    def b2_arrival(h, i):
        return pltpu.make_async_remote_copy(
            src_ref=p2r.at[h, i], dst_ref=p2r.at[h, i],
            send_sem=b2s_sem.at[h, i], recv_sem=b2r_sem.at[h, i],
            device_id=along(h, 1, i), device_id_type=MESH,
        )

    def out_part(h, i):
        return out_hbm.at[pl.ds(h * hr, hr), pl.ds(pl.multiple_of(i * dq, L), dq)]

    def b3_copy(h, i):
        me = place(h, 0)
        return pltpu.make_async_remote_copy(
            src_ref=p3s.at[h], dst_ref=out_part(h, me),
            send_sem=b3s_sem.at[h, i], recv_sem=b3r_sem.at[h, me],
            device_id=along(h, 0, i), device_id_type=MESH,
        )

    def b3_arrival(h, i):
        return pltpu.make_async_remote_copy(
            src_ref=p3s.at[h], dst_ref=out_part(h, i),
            send_sem=b3s_sem.at[h, i], recv_sem=b3r_sem.at[h, i],
            device_id=along(h, 0, i), device_id_type=MESH,
        )

    def partial_block(step, carry):
        for h in range(2):
            i = lax.rem(place(h, 0) + 1 + step, side)
            cols = pl.ds(pl.multiple_of(i * dq, L), dq)
            block = jnp.dot(bm[pl.ds(h * hr, hr), :], ev[:, cols], preferred_element_type=jnp.float32)
            block = block.astype(jnp.bfloat16)

            @pl.when(step < side - 1)
            def _():
                p1s[h, i] = block
                b1_copy(h, i).start()

            @pl.when(step == side - 1)
            def _():
                p1r[h, i] = block

        return carry

    lax.fori_loop(0, side, partial_block, 0)

    for h in range(2):
        me = place(h, 0)
        loop(side, lambda k: b1_arrival(h, lax.rem(me + k, side)).wait_recv())
        p2r[h, place(h, 1)] = added(p1r.at[h], side).astype(jnp.bfloat16)
        mine = place(h, 1)
        loop(side, lambda k: b2_copy(h, lax.rem(mine + k, side)).start())

    dp_finish(2, cs3)
    total = added(cs3, nd)
    cp_ref[...] = (crow[...] - jnp.log2(k_total * total)) * LN2
    back = 1.0 / total
    for t in range(nj):
        col1[pl.ds(t * L, L), :] = to_column(back[t : t + 1, :])

    own = []
    for h in range(2):
        me = place(h, 0)
        mine = place(h, 1)
        loop(side, lambda k: b2_arrival(h, lax.rem(mine + k, side)).wait_recv())
        whole = added(p2r.at[h], side)
        factor = col1[pl.ds(h * hr, hr), :]
        for q in range(dq // L):
            p3s[h, :, q * L : (q + 1) * L] = (whole[:, q * L : (q + 1) * L] * factor).astype(jnp.bfloat16)
        loop(side, lambda k: b3_copy(h, lax.rem(me + k, side)).start())
        keep = pltpu.make_async_copy(p3s.at[h], out_part(h, me), own_sem.at[h])
        keep.start()
        own.append(keep)
    for h in range(2):
        me = place(h, 0)
        loop(side, lambda k: b3_arrival(h, lax.rem(me + k, side)).wait_recv())
        own[h].wait()

    for phase, buf in enumerate((l_all, rho2, rho3)):
        loop(nc, lambda k: cent_copy(phase, buf, k).wait_send())
    for phase, buf in enumerate((lc_all, cs2, cs3)):
        loop(nd, lambda k: dp_copy(phase, buf, k).wait_send())
    for h in range(2):
        me = place(h, 0)
        mine = place(h, 1)
        loop(side, lambda k: b1_copy(h, lax.rem(me + k, side)).wait_send())
        loop(side, lambda k: b2_copy(h, lax.rem(mine + k, side)).wait_send())
        loop(side, lambda k: b3_copy(h, lax.rem(me + k, side)).wait_send())


def on_device(nd, nc, embeddings, centroids, col_start):
    rows, d = embeddings.shape
    kc = centroids.shape[0]
    side = math.isqrt(nd)
    nk, nj = rows // L, kc // L
    hr, dq = kc // 2, d // side
    f32, bf16 = jnp.float32, jnp.bfloat16
    dma = pltpu.SemaphoreType.DMA
    vmem = pl.BlockSpec(memory_space=pltpu.VMEM)
    anywhere = pl.BlockSpec(memory_space=pl.ANY)
    out, row_potential, col_potential = pl.pallas_call(
        functools.partial(kernel, nd, nc, side, float(rows * nd), float(kc * nc)),
        out_shape=(
            jax.ShapeDtypeStruct((kc, d), bf16),
            jax.ShapeDtypeStruct((nk, L), f32),
            jax.ShapeDtypeStruct((nj, L), f32),
        ),
        in_specs=[vmem, anywhere, anywhere],
        out_specs=(anywhere, vmem, vmem),
        scratch_shapes=[
            pltpu.VMEM((kc, d), bf16),
            pltpu.VMEM((rows, d), bf16),
            pltpu.VMEM((nk, kc, L), f32),
            pltpu.VMEM((nk, kc, L), f32),
            pltpu.VMEM((kc, rows), bf16),
            pltpu.VMEM((kc, L), f32),
            pltpu.VMEM((kc, L), f32),
            pltpu.VMEM((kc, L), f32),
            pltpu.VMEM((nk, L), f32),
            pltpu.VMEM((nj, L), f32),
            pltpu.VMEM((nc, nk, L), f32),
            pltpu.VMEM((nc, nk, L), f32),
            pltpu.VMEM((nc, nk, L), f32),
            pltpu.VMEM((nd, nj, L), f32),
            pltpu.VMEM((nd, nj, L), f32),
            pltpu.VMEM((nd, nj, L), f32),
            pltpu.VMEM((2, side, hr, dq), bf16),
            pltpu.VMEM((2, side, hr, dq), bf16),
            pltpu.VMEM((2, hr, dq), bf16),
            pltpu.VMEM((2, side, hr, dq), bf16),
            pltpu.VMEM((2, hr, dq), bf16),
            dma((rows // BLK + 1,)),
            dma((1,)),
            dma((3, nc)),
            dma((3, nc)),
            dma((3, nd)),
            dma((3, nd)),
            dma((2, side)),
            dma((2, side)),
            dma((2, side)),
            dma((2, side)),
            dma((2, side)),
            dma((2, side)),
            dma((2,)),
        ],
        compiler_params=pltpu.CompilerParams(
            collective_id=0, has_side_effects=True, vmem_limit_bytes=56 * 2**20
        ),
        cost_estimate=pl.CostEstimate(
            flops=4 * rows * kc * d, bytes_accessed=2 * (rows + 2 * kc) * d, transcendentals=2 * rows * kc
        ),
        name="sinkhorn",
    )(col_start.reshape(nj, L), centroids, embeddings)
    return out, row_potential.reshape(rows), col_potential.reshape(kc)


def solution(mesh):
    return jax.shard_map(
        functools.partial(on_device, mesh.shape["dp"], mesh.shape["cent"]),
        mesh=mesh,
        in_specs=(P("dp", None), P("cent", None), P("cent")),
        out_specs=(P("cent", None), P("dp"), P("cent")),
        check_vma=False,
    )
```

time: 441 us -> 88.9 us (0.20)
  blocking collectives: 273 us -> 0 us
  waiting for transfers between devices: 105 us -> 0 us
  Pallas kernels: 0 us -> 83.3 us
  other arithmetic: 28.8 us -> 0 us
  matrix products: 13.8 us -> 0 us
  between operations: 14.3 us -> 0.64 us
    psum x1 -> x0, waiting for transfers between devices: 105 us -> none  [on_device(): whole = lax.psum(partial_sums, 'dp')]
    all_gather x6 -> x0, blocking collectives: 101 us -> none  [merged(): everything = jax.tree.map(lambda part: lax.all_gather(part, axis), x)]
    pmax x3 -> x0, blocking collectives: 97.7 us -> none  [on_device(): peak = lax.pmax(local_peak, 'cent')]
    pallas_call x0 -> x1, Pallas kernels: none -> 83.3 us  [on_device(): pl.pallas_call(functools.partial(kernel, nd, nc, side, float(rows * nd),...]
    psum x3 -> x0, blocking collectives: 74.4 us -> none  [on_device(): mass = lax.psum(jnp.sum(jnp.exp(shifted - peak[:, None]), axis=1), 'cent')]
    dot_general x2 -> x0, matrix products: 13.8 us -> none  [the longest x1 7.25 us: on_device(): lax.dot_general(plan, embeddings, (((0,), (0,)), ((), ())), preferred_ele...]
    reduce_max x5 -> x0, other arithmetic: 13.2 us -> none  [the longest x3 8.08 us: on_device(): block_peak = jnp.max(lifted, axis=0)]
    reduce_sum x6 -> x0, other arithmetic: 11.8 us -> none  [the longest x3 9.55 us: on_device(): mass = lax.psum(jnp.sum(jnp.exp(shifted - peak[:, None]), axis=1), 'cent')]
  transfers between devices with their start and end apart: 1 -> 0, of which waited for: 1 -> 0; matrix products, arithmetic and copies ran while one was open for 0% -> 0% of each run, Pallas kernels for 0% -> 0%
where the time goes in v1:
time: 88.9 us; the launch traced here: 88.7 us
  Pallas kernels  83.3 us (94%)
  local copies, waits for them, and re-layouts  4.79 us (5%)
    pallas_call x1, Pallas kernels, on_device(): pl.pallas_call(functools.partial(kernel, nd, nc, side, float(rows * nd),...  83.3 us
    unnamed x3, local copies, waits for them, and re-layouts  4.79 us

profile of v1, /device:TPU:1, one launch (start us, length us, event | category | flops | bytes accessed | tf_op | source)
XLA Modules:
  0.0 88.7 jit_solution(7242777104858597657)
XLA Ops:
  0.6 83.3 %sinkhorn.1 = (bf16[512,1024]{1,0:T(8,128)(2,1)}, f32[16,128]{1,0:T(8,128)}, f32[4,128]{1,0:T(4,128)}) custom-call(f32[4,128]{1,0:T(4,128)} %bitcast.5, bf16[512,1024]{1,0:T(8,128)(2,1)} %c_hbm.1, bf16[2048,1024]{1,0:T(8,128)(2,1)} %e_hbm.1), custom_call_target="tpu_custom_call" | custom-call | flops 4294967296 | bytes 6291456 | tf_op jit(solution)/shard_map/sinkhorn/pallas_call | solution.py:371
  83.9 2.3 %copy.9 = bf16[512,1024]{1,0:T(8,128)(2,1)} copy(bf16[512,1024]{1,0:T(8,128)(2,1)} %get-tuple-element.12) | data formatting | bytes 2097152
  86.2 1.3 %copy.10 = f32[2048]{0:T(1024)} copy(f32[2048]{0:T(1024)} %bitcast.3) | data formatting | bytes 16384
  87.5 1.2 %copy.11 = f32[512]{0:T(512)} copy(f32[512]{0:T(512)} %bitcast.4) | data formatting | bytes 4096

commit v2 on v1

v2 whole, which is shorter than its diff:
```python
import functools
import math

import jax
import jax.numpy as jnp
from jax import lax
from jax.experimental import pallas as pl
from jax.experimental.pallas import tpu as pltpu
from jax.sharding import PartitionSpec as P

MESH = pl.DeviceIdType.MESH
LOG2E = math.log2(math.e)
LN2 = math.log(2.0)
L = 128
BLK = 256
SUB = 32
CHUNKS = 2


def diag_mask():
    return lax.broadcasted_iota(jnp.int32, (L, L), 0) == lax.broadcasted_iota(jnp.int32, (L, L), 1)


def to_column(row):
    spread = jnp.where(diag_mask(), jnp.broadcast_to(row, (L, L)), 0.0)
    return jnp.broadcast_to(jnp.sum(spread, axis=1, keepdims=True), (L, L))


def to_row(column):
    return jnp.sum(jnp.where(diag_mask(), column, 0.0), axis=0, keepdims=True)


def kernel(
    nd, nc, side, n_total, k_total,
    g_ref, c_hbm, e_hbm,
    out_hbm, rp_ref, cp_ref,
    cv, ev, tm, am, bm, gcol, col1, col2, rrow, crow, rsum,
    l_all, rho2, rho3, lc_all, cs2, cs3,
    p1s, p1r, p2r, p3s,
    load_sem, rs_sem, rr_sem, cs_sem, cr_sem,
    b1s_sem, b1r_sem, b2s_sem, b2r_sem, b3s_sem, b3r_sem, own_sem,
):
    kc, d = cv.shape
    nk = tm.shape[0]
    nb = nk * L // BLK
    nj = kc // L
    dp = lax.axis_index("dp")
    ce = lax.axis_index("cent")
    x, y = dp // side, lax.rem(dp, side)

    cent_offsets = sorted(
        ((dz, dc) for dz in range(nc // 2) for dc in range(2) if dz or dc),
        key=lambda o: (-min(o[0], nc // 2 - o[0]), o),
    )
    dp_offsets = sorted(
        ((dx, dy) for dx in range(side) for dy in range(side) if dx or dy),
        key=lambda o: (-min(o[0], side - o[0]) - min(o[1], side - o[1]), o),
    )
    z, core = ce // 2, lax.rem(ce, 2)

    def cent_at(o, sign):
        return lax.rem(z + sign * o[0] + nc // 2, nc // 2) * 2 + lax.rem(core + o[1], 2)

    def dp_at(o, sign):
        return lax.rem(x + sign * o[0] + side, side) * side + lax.rem(y + sign * o[1] + side, side)

    c_load = pltpu.make_async_copy(c_hbm, cv, load_sem.at[nb])
    c_load.start()

    def e_load(b):
        rows = pl.ds(b * BLK, BLK)
        return pltpu.make_async_copy(e_hbm.at[rows], ev.at[rows], load_sem.at[b])

    for b in range(nb):
        e_load(b).start()

    barrier = pltpu.get_barrier_semaphore()
    for o in cent_offsets:
        pl.semaphore_signal(barrier, inc=1, device_id=(dp, cent_at(o, 1)), device_id_type=MESH)
    for o in dp_offsets:
        pl.semaphore_signal(barrier, inc=1, device_id=(dp_at(o, 1), ce), device_id_type=MESH)

    for t in range(nj):
        gcol[pl.ds(t * L, L), :] = to_column(g_ref[pl.ds(t, 1), :] * LOG2E)
    c_load.wait()

    scale = LOG2E / math.sqrt(d)

    def score_block(b, carry):
        e_load(b).wait()
        block = ev[pl.ds(pl.multiple_of(b * BLK, BLK), BLK), :]
        product = lax.dot_general(cv[...], block, (((1,), (1,)), ((), ())), preferred_element_type=jnp.float32)
        product = product * scale
        for h in range(BLK // L):
            tm[b * (BLK // L) + h] = product[:, h * L : (h + 1) * L]
        for h in range(BLK // L):
            k = b * (BLK // L) + h
            peak = jnp.max(tm[k] + gcol[...], axis=0, keepdims=True)
            mass = jnp.sum(jnp.exp2(tm[k] + gcol[...] - peak), axis=0, keepdims=True)
            l_all[ce, pl.ds(k, 1), :] = peak + jnp.log2(mass)
        return carry

    def cent_copy(phase, ref, k):
        return pltpu.make_async_remote_copy(
            src_ref=ref(ce), dst_ref=ref(ce),
            send_sem=rs_sem.at[phase, k], recv_sem=rr_sem.at[phase, k],
            device_id=(dp, cent_at(cent_offsets[k], 1)), device_id_type=MESH,
        )

    def cent_arrival(phase, ref, k):
        fr = cent_at(cent_offsets[k], -1)
        return pltpu.make_async_remote_copy(
            src_ref=ref(fr), dst_ref=ref(fr),
            send_sem=rs_sem.at[phase, k], recv_sem=rr_sem.at[phase, k],
            device_id=(dp, fr), device_id_type=MESH,
        )

    def dp_copy(phase, buf, k):
        return pltpu.make_async_remote_copy(
            src_ref=buf.at[dp], dst_ref=buf.at[dp],
            send_sem=cs_sem.at[phase, k], recv_sem=cr_sem.at[phase, k],
            device_id=(dp_at(dp_offsets[k], 1), ce), device_id_type=MESH,
        )

    def dp_arrival(phase, buf, k):
        fr = dp_at(dp_offsets[k], -1)
        return pltpu.make_async_remote_copy(
            src_ref=buf.at[fr], dst_ref=buf.at[fr],
            send_sem=cs_sem.at[phase, k], recv_sem=cr_sem.at[phase, k],
            device_id=(fr, ce), device_id_type=MESH,
        )

    def cent_start(phase, ref):
        for k in range(nc - 1):
            cent_copy(phase, ref, k).start()

    def cent_finish(phase, ref):
        for k in reversed(range(nc - 1)):
            cent_arrival(phase, ref, k).wait_recv()

    def dp_start(phase, buf):
        for k in range(nd - 1):
            dp_copy(phase, buf, k).start()

    def dp_finish(phase, buf):
        for k in reversed(range(nd - 1)):
            dp_arrival(phase, buf, k).wait_recv()

    early = nk // 2
    part_a = pl.ds(0, early)
    part_b = pl.ds(early, nk - early)

    def l_part(part):
        return lambda s: l_all.at[s, part]

    def whole_of(buf):
        return lambda s: buf.at[s]

    def joined(buf, n):
        peak = buf[0]
        for s in range(1, n):
            peak = jnp.maximum(peak, buf[s])
        total = jnp.exp2(buf[0] - peak)
        for s in range(1, n):
            total = total + jnp.exp2(buf[s] - peak)
        return peak + jnp.log2(total)

    def added(buf, n):
        total = buf[0].astype(jnp.float32)
        for s in range(1, n):
            total = total + buf[s].astype(jnp.float32)
        return total

    lax.fori_loop(0, early * L // BLK, score_block, 0)
    pl.semaphore_wait(barrier, nc - 1 + nd - 1)
    cent_start(0, l_part(part_a))
    lax.fori_loop(early * L // BLK, nb, score_block, 0)
    cent_start(1, l_part(part_b))
    cent_finish(0, l_part(part_a))
    cent_finish(1, l_part(part_b))

    rrow[...] = -math.log2(n_total) - joined(l_all, nc)

    def first_columns(jb, carry):
        rows = pl.ds(pl.multiple_of(jb * SUB, SUB), SUB)
        peak = tm[0, rows, :] + rrow[pl.ds(0, 1), :]
        for k in range(1, nk):
            peak = jnp.maximum(peak, tm[k, rows, :] + rrow[pl.ds(k, 1), :])
        peak = jnp.broadcast_to(jnp.max(peak, axis=1, keepdims=True), (SUB, L))
        mass = jnp.zeros((SUB, L), jnp.float32)
        for k in range(nk):
            value = jnp.exp2(tm[k, rows, :] + rrow[pl.ds(k, 1), :] - peak)
            am[k, rows, :] = value
            mass = mass + value
        col1[rows, :] = peak
        col2[rows, :] = jnp.broadcast_to(jnp.sum(mass, axis=1, keepdims=True), (SUB, L))
        return carry

    lax.fori_loop(0, kc // SUB, first_columns, 0)
    for t in range(nj):
        top = to_row(col1[pl.ds(t * L, L), :])
        crow[pl.ds(t, 1), :] = top
        lc_all[dp, pl.ds(t, 1), :] = top + jnp.log2(to_row(col2[pl.ds(t * L, L), :]))
    dp_start(0, lc_all)
    dp_finish(0, lc_all)
    g_one = -math.log2(k_total) - joined(lc_all, nd)
    lift = jnp.exp2(crow[...] + g_one)
    crow[...] = g_one
    for t in range(nj):
        col1[pl.ds(t * L, L), :] = to_column(lift[t : t + 1, :])

    def second_rows(k, carry):
        value = am[k] * col1[...]
        am[k] = value
        rsum[pl.ds(k, 1), :] = jnp.sum(value, axis=0, keepdims=True)
        return carry

    lax.fori_loop(0, nk, second_rows, 0)
    rho2[ce] = rsum[...].astype(rho2.dtype)
    cent_start(2, whole_of(rho2))
    cent_finish(2, whole_of(rho2))
    u_two = 1.0 / (n_total * added(rho2, nc))

    def column_sums(u, target, keep):
        def body(jb, carry):
            rows = pl.ds(pl.multiple_of(jb * SUB, SUB), SUB)
            mass = jnp.zeros((SUB, L), jnp.float32)
            for k in range(nk):
                value = am[k, rows, :] * u[k : k + 1, :]
                if keep:
                    bm[rows, k * L : (k + 1) * L] = value.astype(jnp.bfloat16)
                mass = mass + value
            col2[rows, :] = jnp.broadcast_to(jnp.sum(mass, axis=1, keepdims=True), (SUB, L))
            return carry

        lax.fori_loop(0, kc // SUB, body, 0)
        for t in range(nj):
            target[dp, pl.ds(t, 1), :] = to_row(col2[pl.ds(t * L, L), :])

    column_sums(u_two, cs2, False)
    dp_start(1, cs2)
    dp_finish(1, cs2)
    v_two = 1.0 / (k_total * added(cs2, nd))
    for t in range(nj):
        col1[pl.ds(t * L, L), :] = to_column(v_two[t : t + 1, :])

    def third_rows(k, carry):
        rho3[ce, pl.ds(k, 1), :] = jnp.sum(am[k] * col1[...], axis=0, keepdims=True)
        return carry

    lax.fori_loop(0, nk, third_rows, 0)
    cent_start(3, whole_of(rho3))
    cent_finish(3, whole_of(rho3))
    u_three = 1.0 / (n_total * added(rho3, nc))
    rp_ref[...] = (rrow[...] + jnp.log2(u_three)) * LN2

    column_sums(u_three, cs3, True)
    dp_start(2, cs3)

    hr = kc // 2
    cr = hr // CHUNKS
    dq = d // side
    here = (x, y)
    offsets = sorted(range(1, side), key=lambda o: -min(o, side - o))

    def along(h, stage, i):
        if (h + stage) % 2 == 0:
            return (i * side + y, ce)
        return (x * side + i, ce)

    def place(h, stage, o=0):
        return lax.rem(here[(h + stage) % 2] + o + side, side)

    def chunk(c):
        return pl.ds(c * cr, cr)

    def b1(h, c, n, to, fr):
        return pltpu.make_async_remote_copy(
            src_ref=p1s.at[h, to, chunk(c)], dst_ref=p1r.at[h, fr, chunk(c)],
            send_sem=b1s_sem.at[h, c, n], recv_sem=b1r_sem.at[h, c, n],
            device_id=along(h, 0, to), device_id_type=MESH,
        )

    def b2(h, c, n, to, fr):
        return pltpu.make_async_remote_copy(
            src_ref=p2r.at[h, fr, chunk(c)], dst_ref=p2r.at[h, fr, chunk(c)],
            send_sem=b2s_sem.at[h, c, n], recv_sem=b2r_sem.at[h, c, n],
            device_id=along(h, 1, to), device_id_type=MESH,
        )

    def out_part(h, c, i):
        return out_hbm.at[pl.ds(h * hr + c * cr, cr), pl.ds(pl.multiple_of(i * dq, L), dq)]

    def b3(h, c, n, to, fr):
        return pltpu.make_async_remote_copy(
            src_ref=p3s.at[h, chunk(c)], dst_ref=out_part(h, c, fr),
            send_sem=b3s_sem.at[h, c, n], recv_sem=b3r_sem.at[h, c, n],
            device_id=along(h, 0, to), device_id_type=MESH,
        )

    def sending(copy, stage, h, c, n):
        return copy(h, c, n, place(h, stage, offsets[n]), place(h, stage))

    def arriving(copy, stage, h, c, n):
        return copy(h, c, n, place(h, stage), place(h, stage, -offsets[n]))

    def block_of(h, c, i):
        cols = pl.ds(pl.multiple_of(i * dq, L), dq)
        rows = pl.ds(h * hr + c * cr, cr)
        return jnp.dot(bm[rows, :], ev[:, cols], preferred_element_type=jnp.float32).astype(jnp.bfloat16)

    pieces = [(c, h) for c in range(CHUNKS) for h in range(2)]
    for c in range(CHUNKS):
        for n in range(side - 1):
            for h in range(2):
                p1s[h, place(h, 0, offsets[n]), chunk(c)] = block_of(h, c, place(h, 0, offsets[n]))
                sending(b1, 0, h, c, n).start()
        for h in range(2):
            p1r[h, place(h, 0), chunk(c)] = block_of(h, c, place(h, 0))

    def summed(buf, h, c):
        total = buf[h, 0, chunk(c)].astype(jnp.float32)
        for i in range(1, side):
            total = total + buf[h, i, chunk(c)].astype(jnp.float32)
        return total

    for c, h in pieces:
        for n in reversed(range(side - 1)):
            arriving(b1, 0, h, c, n).wait_recv()
        p2r[h, place(h, 1), chunk(c)] = summed(p1r, h, c).astype(jnp.bfloat16)
        for n in range(side - 1):
            sending(b2, 1, h, c, n).start()

    dp_finish(2, cs3)
    total = added(cs3, nd)
    cp_ref[...] = (crow[...] - jnp.log2(k_total * total)) * LN2
    back = 1.0 / total
    for t in range(nj):
        col1[pl.ds(t * L, L), :] = to_column(back[t : t + 1, :])

    own = []
    for c, h in pieces:
        for n in reversed(range(side - 1)):
            arriving(b2, 1, h, c, n).wait_recv()
        whole = summed(p2r, h, c)
        factor = col1[pl.ds(h * hr + c * cr, cr), :]
        for q in range(dq // L):
            p3s[h, chunk(c), q * L : (q + 1) * L] = (whole[:, q * L : (q + 1) * L] * factor).astype(jnp.bfloat16)
        for n in range(side - 1):
            sending(b3, 0, h, c, n).start()
        keep = pltpu.make_async_copy(p3s.at[h, chunk(c)], out_part(h, c, place(h, 0)), own_sem.at[h, c])
        keep.start()
        own.append(keep)

    for phase, ref in enumerate((l_part(part_a), l_part(part_b), whole_of(rho2), whole_of(rho3))):
        for k in range(nc - 1):
            cent_copy(phase, ref, k).wait_send()
    for phase, buf in enumerate((lc_all, cs2, cs3)):
        for k in range(nd - 1):
            dp_copy(phase, buf, k).wait_send()
    for c, h in pieces:
        for n in range(side - 1):
            sending(b1, 0, h, c, n).wait_send()
            sending(b2, 1, h, c, n).wait_send()
    for c, h in pieces:
        for n in reversed(range(side - 1)):
            arriving(b3, 0, h, c, n).wait_recv()
    for keep in own:
        keep.wait()
    for c, h in pieces:
        for n in range(side - 1):
            sending(b3, 0, h, c, n).wait_send()


def closing(c_in, r_in, k_in, c_out, r_out, k_out, c_v, r_v, k_v, in_sem, out_sem):
    step = c_v.shape[0] // 4
    parts = [(c_in.at[pl.ds(i * step, step)], c_v.at[pl.ds(i * step, step)], c_out.at[pl.ds(i * step, step)]) for i in range(4)]
    parts += [(r_in, r_v, r_out), (k_in, k_v, k_out)]
    arriving = [pltpu.make_async_copy(a, b, in_sem.at[i]) for i, (a, b, _) in enumerate(parts)]
    leaving = [pltpu.make_async_copy(b, c, out_sem.at[i]) for i, (_, b, c) in enumerate(parts)]
    for copy in arriving:
        copy.start()
    for a, b in zip(arriving, leaving):
        a.wait()
        b.start()
    for copy in leaving:
        copy.wait()


def on_device(nd, nc, embeddings, centroids, col_start):
    rows, d = embeddings.shape
    kc = centroids.shape[0]
    side = math.isqrt(nd)
    nk, nj = rows // L, kc // L
    hr, dq = kc // 2, d // side
    f32, bf16 = jnp.float32, jnp.bfloat16
    dma = pltpu.SemaphoreType.DMA
    vmem = pl.BlockSpec(memory_space=pltpu.VMEM)
    anywhere = pl.BlockSpec(memory_space=pl.ANY)
    out, row_potential, col_potential = pl.pallas_call(
        functools.partial(kernel, nd, nc, side, float(rows * nd), float(kc * nc)),
        out_shape=(
            jax.ShapeDtypeStruct((kc, d), bf16),
            jax.ShapeDtypeStruct((nk, L), f32),
            jax.ShapeDtypeStruct((nj, L), f32),
        ),
        in_specs=[vmem, anywhere, anywhere],
        out_specs=(anywhere, vmem, vmem),
        scratch_shapes=[
            pltpu.VMEM((kc, d), bf16),
            pltpu.VMEM((rows, d), bf16),
            pltpu.VMEM((nk, kc, L), f32),
            pltpu.VMEM((nk, kc, L), f32),
            pltpu.VMEM((kc, rows), bf16),
            pltpu.VMEM((kc, L), f32),
            pltpu.VMEM((kc, L), f32),
            pltpu.VMEM((kc, L), f32),
            pltpu.VMEM((nk, L), f32),
            pltpu.VMEM((nj, L), f32),
            pltpu.VMEM((nk, L), f32),
            pltpu.VMEM((nc, nk, L), f32),
            pltpu.VMEM((nc, nk, L), bf16),
            pltpu.VMEM((nc, nk, L), f32),
            pltpu.VMEM((nd, nj, L), f32),
            pltpu.VMEM((nd, nj, L), f32),
            pltpu.VMEM((nd, nj, L), f32),
            pltpu.VMEM((2, side, hr, dq), bf16),
            pltpu.VMEM((2, side, hr, dq), bf16),
            pltpu.VMEM((2, side, hr, dq), bf16),
            pltpu.VMEM((2, hr, dq), bf16),
            dma((rows // BLK + 1,)),
            dma((4, nc - 1)),
            dma((4, nc - 1)),
            dma((3, nd - 1)),
            dma((3, nd - 1)),
            dma((2, CHUNKS, side - 1)),
            dma((2, CHUNKS, side - 1)),
            dma((2, CHUNKS, side - 1)),
            dma((2, CHUNKS, side - 1)),
            dma((2, CHUNKS, side - 1)),
            dma((2, CHUNKS, side - 1)),
            dma((2, CHUNKS)),
        ],
        compiler_params=pltpu.CompilerParams(
            collective_id=0, has_side_effects=True, vmem_limit_bytes=56 * 2**20
        ),
        cost_estimate=pl.CostEstimate(
            flops=4 * rows * kc * d, bytes_accessed=2 * (rows + 2 * kc) * d, transcendentals=2 * rows * kc
        ),
        name="sinkhorn",
    )(col_start.reshape(nj, L), centroids, embeddings)
    parts = (out, row_potential, col_potential)
    out, row_potential, col_potential = pl.pallas_call(
        closing,
        out_shape=tuple(jax.ShapeDtypeStruct(part.shape, part.dtype) for part in parts),
        in_specs=[anywhere] * 3,
        out_specs=(anywhere,) * 3,
        scratch_shapes=[pltpu.VMEM(part.shape, part.dtype) for part in parts] + [dma((6,)), dma((6,))],
        name="closing",
    )(*parts)
    return out, row_potential.reshape(rows), col_potential.reshape(kc)


def solution(mesh):
    return jax.shard_map(
        functools.partial(on_device, mesh.shape["dp"], mesh.shape["cent"]),
        mesh=mesh,
        in_specs=(P("dp", None), P("cent", None), P("cent")),
        out_specs=(P("cent", None), P("dp"), P("cent")),
        check_vma=False,
    )
```

time: 88.9 us -> 75.1 us (0.84)
  Pallas kernels: 83.3 us -> 74.3 us
  local copies, waits for them, and re-layouts: 4.79 us -> 0 us
    pallas_call x1, Pallas kernels: 83.3 us -> 72.3 us  [on_device(): pl.pallas_call(functools.partial(kernel, nd, nc, side, float(rows * nd),...]
    unnamed x3 -> x0, local copies, waits for them, and re-layouts: 4.79 us -> none
    pallas_call x0 -> x1, Pallas kernels: none -> 2.02 us  [on_device(): pl.pallas_call(closing, out_shape=tuple((jax.ShapeDtypeStruct(part.shape,...]
where the time goes in v2:
time: 75.1 us; the launch traced here: 74.9 us
  Pallas kernels  74.3 us (99%)
    pallas_call x1, Pallas kernels, on_device(): pl.pallas_call(functools.partial(kernel, nd, nc, side, float(rows * nd),...  72.3 us
    pallas_call x1, Pallas kernels, on_device(): pl.pallas_call(closing, out_shape=tuple((jax.ShapeDtypeStruct(part.shape,...  2.02 us

profile of v2, /device:TPU:1, one launch (start us, length us, event | category | flops | bytes accessed | tf_op | source)
XLA Modules:
  0.0 74.9 jit_solution(9156196064096933504)
XLA Ops:
  0.6 72.3 %sinkhorn.1 = (bf16[512,1024]{1,0:T(8,128)(2,1)}, f32[16,128]{1,0:T(8,128)}, f32[4,128]{1,0:T(4,128)}) custom-call(f32[4,128]{1,0:T(4,128)} %bitcast.4, bf16[512,1024]{1,0:T(8,128)(2,1)} %c_hbm.1, bf16[2048,1024]{1,0:T(8,128)(2,1)} %e_hbm.1), custom_call_target="tpu_custom_call" | custom-call | flops 4294967296 | bytes 6291456 | tf_op jit(solution)/shard_map/sinkhorn/pallas_call | solution.py:400
  72.9 2.0 %closing.1 = (bf16[512,1024]{1,0:T(8,128)(2,1)}, f32[16,128]{1,0:T(8,128)}, f32[4,128]{1,0:T(4,128)}) custom-call(bf16[512,1024]{1,0:T(8,128)(2,1)} %get-tuple-element.9.c_in, f32[16,128]{1,0:T(8,128)} %get-tuple-element.10.r_in, f32[4,128]{1,0:T(4,128)} %get-tuple-element.11.k_in), custom_call_target="tpu_custom_call" | custom-call | tf_op jit(solution)/shard_map/closing/pallas_call | solution.py:453

commit v3 on v2

--- a/solution.py
+++ b/solution.py
@@ -13,7 +13,8 @@
 LN2 = math.log(2.0)
 L = 128
 BLK = 256
-SUB = 32
+SUB = 128
+SUB1 = 64
 CHUNKS = 2
 
 
@@ -28,6 +29,13 @@
 
 def to_row(column):
     return jnp.sum(jnp.where(diag_mask(), column, 0.0), axis=0, keepdims=True)
+
+
+def fold(x, act):
+    while x.shape[0] > 8:
+        half = x.shape[0] // 2
+        x = act(x[:half], x[half:])
+    return x
 
 
 def kernel(
@@ -95,8 +103,8 @@
             tm[b * (BLK // L) + h] = product[:, h * L : (h + 1) * L]
         for h in range(BLK // L):
             k = b * (BLK // L) + h
-            peak = jnp.max(tm[k] + gcol[...], axis=0, keepdims=True)
-            mass = jnp.sum(jnp.exp2(tm[k] + gcol[...] - peak), axis=0, keepdims=True)
+            peak = jnp.max(fold(tm[k] + gcol[...], jnp.maximum), axis=0, keepdims=True)
+            mass = jnp.sum(fold(jnp.exp2(tm[k] + gcol[...] - peak), jnp.add), axis=0, keepdims=True)
             l_all[ce, pl.ds(k, 1), :] = peak + jnp.log2(mass)
         return carry
 
@@ -182,21 +190,21 @@
     rrow[...] = -math.log2(n_total) - joined(l_all, nc)
 
     def first_columns(jb, carry):
-        rows = pl.ds(pl.multiple_of(jb * SUB, SUB), SUB)
+        rows = pl.ds(pl.multiple_of(jb * SUB1, SUB1), SUB1)
         peak = tm[0, rows, :] + rrow[pl.ds(0, 1), :]
         for k in range(1, nk):
             peak = jnp.maximum(peak, tm[k, rows, :] + rrow[pl.ds(k, 1), :])
-        peak = jnp.broadcast_to(jnp.max(peak, axis=1, keepdims=True), (SUB, L))
-        mass = jnp.zeros((SUB, L), jnp.float32)
+        peak = jnp.broadcast_to(jnp.max(peak, axis=1, keepdims=True), (SUB1, L))
+        mass = jnp.zeros((SUB1, L), jnp.float32)
         for k in range(nk):
             value = jnp.exp2(tm[k, rows, :] + rrow[pl.ds(k, 1), :] - peak)
             am[k, rows, :] = value
             mass = mass + value
         col1[rows, :] = peak
-        col2[rows, :] = jnp.broadcast_to(jnp.sum(mass, axis=1, keepdims=True), (SUB, L))
+        col2[rows, :] = jnp.broadcast_to(jnp.sum(mass, axis=1, keepdims=True), (SUB1, L))
         return carry
 
-    lax.fori_loop(0, kc // SUB, first_columns, 0)
+    lax.fori_loop(0, kc // SUB1, first_columns, 0, unroll=2)
     for t in range(nj):
         top = to_row(col1[pl.ds(t * L, L), :])
         crow[pl.ds(t, 1), :] = top
@@ -212,10 +220,10 @@
     def second_rows(k, carry):
         value = am[k] * col1[...]
         am[k] = value
-        rsum[pl.ds(k, 1), :] = jnp.sum(value, axis=0, keepdims=True)
+        rsum[pl.ds(k, 1), :] = jnp.sum(fold(value, jnp.add), axis=0, keepdims=True)
         return carry
 
-    lax.fori_loop(0, nk, second_rows, 0)
+    lax.fori_loop(0, nk, second_rows, 0, unroll=2)
     rho2[ce] = rsum[...].astype(rho2.dtype)
     cent_start(2, whole_of(rho2))
     cent_finish(2, whole_of(rho2))
@@ -233,7 +241,7 @@
             col2[rows, :] = jnp.broadcast_to(jnp.sum(mass, axis=1, keepdims=True), (SUB, L))
             return carry
 
-        lax.fori_loop(0, kc // SUB, body, 0)
+        lax.fori_loop(0, kc // SUB, body, 0, unroll=2)
         for t in range(nj):
             target[dp, pl.ds(t, 1), :] = to_row(col2[pl.ds(t * L, L), :])
 
@@ -245,10 +253,10 @@
         col1[pl.ds(t * L, L), :] = to_column(v_two[t : t + 1, :])
 
     def third_rows(k, carry):
-        rho3[ce, pl.ds(k, 1), :] = jnp.sum(am[k] * col1[...], axis=0, keepdims=True)
+        rho3[ce, pl.ds(k, 1), :] = jnp.sum(fold(am[k] * col1[...], jnp.add), axis=0, keepdims=True)
         return carry
 
-    lax.fori_loop(0, nk, third_rows, 0)
+    lax.fori_loop(0, nk, third_rows, 0, unroll=2)
     cent_start(3, whole_of(rho3))
     cent_finish(3, whole_of(rho3))
     u_three = 1.0 / (n_total * added(rho3, nc))

time: 75.1 us -> 68.2 us (0.908)
  Pallas kernels: 74.3 us -> 67.4 us
    pallas_call x1, Pallas kernels: 72.3 us -> 65.4 us  [on_device(): pl.pallas_call(functools.partial(kernel, nd, nc, side, float(rows * nd),...]
where the time goes in v3:
time: 68.2 us; the launch traced here: 68.1 us
  Pallas kernels  67.4 us (99%)
    pallas_call x1, Pallas kernels, on_device(): pl.pallas_call(functools.partial(kernel, nd, nc, side, float(rows * nd),...  65.4 us
    pallas_call x1, Pallas kernels, on_device(): pl.pallas_call(closing, out_shape=tuple((jax.ShapeDtypeStruct(part.shape,...  2.02 us

profile of v3, /device:TPU:1, one launch (start us, length us, event | category | flops | bytes accessed | tf_op | source)
XLA Modules:
  0.0 68.1 jit_solution(11405196401206798987)
XLA Ops:
  0.6 65.4 %sinkhorn.1 = (bf16[512,1024]{1,0:T(8,128)(2,1)}, f32[16,128]{1,0:T(8,128)}, f32[4,128]{1,0:T(4,128)}) custom-call(f32[4,128]{1,0:T(4,128)} %bitcast.4, bf16[512,1024]{1,0:T(8,128)(2,1)} %c_hbm.1, bf16[2048,1024]{1,0:T(8,128)(2,1)} %e_hbm.1), custom_call_target="tpu_custom_call" | custom-call | flops 4294967296 | bytes 6291456 | tf_op jit(solution)/shard_map/sinkhorn/pallas_call | solution.py:408
  66.0 2.0 %closing.1 = (bf16[512,1024]{1,0:T(8,128)(2,1)}, f32[16,128]{1,0:T(8,128)}, f32[4,128]{1,0:T(4,128)}) custom-call(bf16[512,1024]{1,0:T(8,128)(2,1)} %get-tuple-element.9.c_in, f32[16,128]{1,0:T(8,128)} %get-tuple-element.10.r_in, f32[4,128]{1,0:T(4,128)} %get-tuple-element.11.k_in), custom_call_target="tpu_custom_call" | custom-call | tf_op jit(solution)/shard_map/closing/pallas_call | solution.py:461

commit v4 on v3

--- a/solution.py
+++ b/solution.py
@@ -16,6 +16,8 @@
 SUB = 128
 SUB1 = 64
 CHUNKS = 2
+MATS = 2
+PIECES = 4
 
 
 def diag_mask():
@@ -40,9 +42,9 @@
 
 def kernel(
     nd, nc, side, n_total, k_total,
-    g_ref, c_hbm, e_hbm,
+    g_hbm, c_hbm, e_hbm,
     out_hbm, rp_ref, cp_ref,
-    cv, ev, tm, am, bm, gcol, col1, col2, rrow, crow, rsum,
+    g_ref, cv, ev, tm, am, bm, gcol, col1, col2, rrow, crow, rsum,
     l_all, rho2, rho3, lc_all, cs2, cs3,
     p1s, p1r, p2r, p3s,
     load_sem, rs_sem, rr_sem, cs_sem, cr_sem,
@@ -73,7 +75,9 @@
         return lax.rem(x + sign * o[0] + side, side) * side + lax.rem(y + sign * o[1] + side, side)
 
     c_load = pltpu.make_async_copy(c_hbm, cv, load_sem.at[nb])
+    g_load = pltpu.make_async_copy(g_hbm, g_ref, load_sem.at[nb + 1])
     c_load.start()
+    g_load.start()
 
     def e_load(b):
         rows = pl.ds(b * BLK, BLK)
@@ -88,6 +92,7 @@
     for o in dp_offsets:
         pl.semaphore_signal(barrier, inc=1, device_id=(dp_at(o, 1), ce), device_id_type=MESH)
 
+    g_load.wait()
     for t in range(nj):
         gcol[pl.ds(t * L, L), :] = to_column(g_ref[pl.ds(t, 1), :] * LOG2E)
     c_load.wait()
@@ -229,23 +234,23 @@
     cent_finish(2, whole_of(rho2))
     u_two = 1.0 / (n_total * added(rho2, nc))
 
-    def column_sums(u, target, keep):
-        def body(jb, carry):
-            rows = pl.ds(pl.multiple_of(jb * SUB, SUB), SUB)
-            mass = jnp.zeros((SUB, L), jnp.float32)
-            for k in range(nk):
-                value = am[k, rows, :] * u[k : k + 1, :]
-                if keep:
-                    bm[rows, k * L : (k + 1) * L] = value.astype(jnp.bfloat16)
-                mass = mass + value
-            col2[rows, :] = jnp.broadcast_to(jnp.sum(mass, axis=1, keepdims=True), (SUB, L))
-            return carry
-
-        lax.fori_loop(0, kc // SUB, body, 0, unroll=2)
+    def column_block(u, start, size, keep):
+        rows = pl.ds(start, size)
+        mass = jnp.zeros((size, L), jnp.float32)
+        for k in range(nk):
+            value = am[k, rows, :] * u[k : k + 1, :]
+            if keep:
+                bm[rows, k * L : (k + 1) * L] = value.astype(jnp.bfloat16)
+            mass = mass + value
+        col2[rows, :] = jnp.broadcast_to(jnp.sum(mass, axis=1, keepdims=True), (size, L))
+
+    def column_rows(target):
         for t in range(nj):
             target[dp, pl.ds(t, 1), :] = to_row(col2[pl.ds(t * L, L), :])
 
-    column_sums(u_two, cs2, False)
+    for start in range(0, kc, SUB):
+        column_block(u_two, start, SUB, False)
+    column_rows(cs2)
     dp_start(1, cs2)
     dp_finish(1, cs2)
     v_two = 1.0 / (k_total * added(cs2, nd))
@@ -262,8 +267,6 @@
     u_three = 1.0 / (n_total * added(rho3, nc))
     rp_ref[...] = (rrow[...] + jnp.log2(u_three)) * LN2
 
-    column_sums(u_three, cs3, True)
-    dp_start(2, cs3)
 
     hr = kc // 2
     cr = hr // CHUNKS
@@ -312,19 +315,34 @@
     def arriving(copy, stage, h, c, n):
         return copy(h, c, n, place(h, stage), place(h, stage, -offsets[n]))
 
-    def block_of(h, c, i):
-        cols = pl.ds(pl.multiple_of(i * dq, L), dq)
-        rows = pl.ds(h * hr + c * cr, cr)
-        return jnp.dot(bm[rows, :], ev[:, cols], preferred_element_type=jnp.float32).astype(jnp.bfloat16)
-
     pieces = [(c, h) for c in range(CHUNKS) for h in range(2)]
-    for c in range(CHUNKS):
+    per = CHUNKS // MATS
+    mr = hr // MATS
+
+    def product_step(m, n, o):
+        for h in range(2):
+            i = place(h, 0, o)
+            cols = pl.ds(pl.multiple_of(i * dq, L), dq)
+            rows = pl.ds(m * mr, mr)
+            block = jnp.dot(bm[pl.ds(h * hr + m * mr, mr), :], ev[:, cols], preferred_element_type=jnp.float32)
+            block = block.astype(jnp.bfloat16)
+            if n is None:
+                p1r[h, i, rows] = block
+            else:
+                p1s[h, i, rows] = block
+                for c in range(m * per, (m + 1) * per):
+                    b1(h, c, n, i, place(h, 0)).start()
+
+    for m in range(MATS):
+        for h in range(2):
+            for start in range(h * hr + m * mr, h * hr + (m + 1) * mr, min(SUB, mr)):
+                column_block(u_three, start, min(SUB, mr), True)
+        if m == MATS - 1:
+            column_rows(cs3)
+            dp_start(2, cs3)
         for n in range(side - 1):
-            for h in range(2):
-                p1s[h, place(h, 0, offsets[n]), chunk(c)] = block_of(h, c, place(h, 0, offsets[n]))
-                sending(b1, 0, h, c, n).start()
-        for h in range(2):
-            p1r[h, place(h, 0), chunk(c)] = block_of(h, c, place(h, 0))
+            product_step(m, n, offsets[n])
+        product_step(m, None, 0)
 
     def summed(buf, h, c):
         total = buf[h, 0, chunk(c)].astype(jnp.float32)
@@ -380,18 +398,14 @@
             sending(b3, 0, h, c, n).wait_send()
 
 
-def closing(c_in, r_in, k_in, c_out, r_out, k_out, c_v, r_v, k_v, in_sem, out_sem):
-    step = c_v.shape[0] // 4
-    parts = [(c_in.at[pl.ds(i * step, step)], c_v.at[pl.ds(i * step, step)], c_out.at[pl.ds(i * step, step)]) for i in range(4)]
-    parts += [(r_in, r_v, r_out), (k_in, k_v, k_out)]
-    arriving = [pltpu.make_async_copy(a, b, in_sem.at[i]) for i, (a, b, _) in enumerate(parts)]
-    leaving = [pltpu.make_async_copy(b, c, out_sem.at[i]) for i, (_, b, c) in enumerate(parts)]
-    for copy in arriving:
+def closing(c_in, r_in, k_in, c_out, r_out, k_out, sem):
+    step = c_in.shape[0] // PIECES
+    pairs = [(c_in.at[pl.ds(i * step, step)], c_out.at[pl.ds(i * step, step)]) for i in range(PIECES)]
+    pairs += [(r_in, r_out), (k_in, k_out)]
+    copies = [pltpu.make_async_copy(a, b, sem.at[i]) for i, (a, b) in enumerate(pairs)]
+    for copy in copies:
         copy.start()
-    for a, b in zip(arriving, leaving):
-        a.wait()
-        b.start()
-    for copy in leaving:
+    for copy in copies:
         copy.wait()
 
 
@@ -408,13 +422,14 @@
     out, row_potential, col_potential = pl.pallas_call(
         functools.partial(kernel, nd, nc, side, float(rows * nd), float(kc * nc)),
         out_shape=(
-            jax.ShapeDtypeStruct((kc, d), bf16),
-            jax.ShapeDtypeStruct((nk, L), f32),
-            jax.ShapeDtypeStruct((nj, L), f32),
+            pltpu.VMEM((kc, d), bf16),
+            pltpu.VMEM((nk, L), f32),
+            pltpu.VMEM((nj, L), f32),
         ),
-        in_specs=[vmem, anywhere, anywhere],
-        out_specs=(anywhere, vmem, vmem),
+        in_specs=[anywhere] * 3,
+        out_specs=(vmem, vmem, vmem),
         scratch_shapes=[
+            pltpu.VMEM((nj, L), f32),
             pltpu.VMEM((kc, d), bf16),
             pltpu.VMEM((rows, d), bf16),
             pltpu.VMEM((nk, kc, L), f32),
@@ -436,7 +451,7 @@
             pltpu.VMEM((2, side, hr, dq), bf16),
             pltpu.VMEM((2, side, hr, dq), bf16),
             pltpu.VMEM((2, hr, dq), bf16),
-            dma((rows // BLK + 1,)),
+            dma((rows // BLK + 2,)),
             dma((4, nc - 1)),
             dma((4, nc - 1)),
             dma((3, nd - 1)),
@@ -450,7 +465,7 @@
             dma((2, CHUNKS)),
         ],
         compiler_params=pltpu.CompilerParams(
-            collective_id=0, has_side_effects=True, vmem_limit_bytes=56 * 2**20
+            collective_id=0, has_side_effects=True, vmem_limit_bytes=125 * 2**19
         ),
         cost_estimate=pl.CostEstimate(
             flops=4 * rows * kc * d, bytes_accessed=2 * (rows + 2 * kc) * d, transcendentals=2 * rows * kc
@@ -461,11 +476,11 @@
     out, row_potential, col_potential = pl.pallas_call(
         closing,
         out_shape=tuple(jax.ShapeDtypeStruct(part.shape, part.dtype) for part in parts),
-        in_specs=[anywhere] * 3,
+        in_specs=[vmem] * 3,
         out_specs=(anywhere,) * 3,
-        scratch_shapes=[pltpu.VMEM(part.shape, part.dtype) for part in parts] + [dma((6,)), dma((6,))],
+        scratch_shapes=[dma((PIECES + 2,))],
         name="closing",
-    )(*parts)
+    )(*(pltpu.with_memory_space_constraint(part, pltpu.VMEM) for part in parts))
     return out, row_potential.reshape(rows), col_potential.reshape(kc)
 
 

time: 68.2 us -> 64.8 us (0.950)
  Pallas kernels: 67.4 us -> 64.1 us
    pallas_call x1, Pallas kernels: 65.4 us -> 63.1 us  [on_device(): pl.pallas_call(functools.partial(kernel, nd, nc, side, float(rows * nd),...]
    pallas_call x1, Pallas kernels: 2.02 us -> 1.02 us  [on_device(): pl.pallas_call(closing, out_shape=tuple((jax.ShapeDtypeStruct(part.shape,...]
where the time goes in v4:
time: 64.8 us; the launch traced here: 64.7 us
  Pallas kernels  64.1 us (99%)
    pallas_call x1, Pallas kernels, on_device(): pl.pallas_call(functools.partial(kernel, nd, nc, side, float(rows * nd),...  63.1 us

profile of v4, /device:TPU:1, one launch (start us, length us, event | category | flops | bytes accessed | tf_op | source)
XLA Modules:
  0.0 64.7 jit_solution(304784657064847673)
XLA Ops:
  0.6 63.1 %sinkhorn.1 = (bf16[512,1024]{1,0:T(8,128)(2,1)S(1)}, f32[16,128]{1,0:T(8,128)S(1)}, f32[4,128]{1,0:T(4,128)S(1)}) custom-call(f32[4,128]{1,0:T(4,128)} %bitcast.4, bf16[512,1024]{1,0:T(8,128)(2,1)} %c_hbm.1, bf16[2048,1024]{1,0:T(8,128)(2,1)} %e_hbm.1), custom_call_target="tpu_custom_call" | custom-call | flops 4294967296 | bytes 6291456 | tf_op jit(solution)/shard_map/sinkhorn/pallas_call | solution.py:422
  63.7 1.0 %closing.1 = (bf16[512,1024]{1,0:T(8,128)(2,1)}, f32[16,128]{1,0:T(8,128)}, f32[4,128]{1,0:T(4,128)}) custom-call(bf16[512,1024]{1,0:T(8,128)(2,1)S(1)} %get-tuple-element.9.c_in, f32[16,128]{1,0:T(8,128)S(1)} %get-tuple-element.10.r_in, f32[4,128]{1,0:T(4,128)S(1)} %get-tuple-element.11.k_in), custom_call_target="tpu_custom_call" | custom-call | tf_op jit(solution)/shard_map/closing/pallas_call | solution.py:476

commit v5 on v4

--- a/solution.py
+++ b/solution.py
@@ -258,10 +258,11 @@
         col1[pl.ds(t * L, L), :] = to_column(v_two[t : t + 1, :])
 
     def third_rows(k, carry):
-        rho3[ce, pl.ds(k, 1), :] = jnp.sum(fold(am[k] * col1[...], jnp.add), axis=0, keepdims=True)
+        rsum[pl.ds(k, 1), :] = jnp.sum(fold(am[k] * col1[...], jnp.add), axis=0, keepdims=True)
         return carry
 
     lax.fori_loop(0, nk, third_rows, 0, unroll=2)
+    rho3[ce] = rsum[...].astype(rho3.dtype)
     cent_start(3, whole_of(rho3))
     cent_finish(3, whole_of(rho3))
     u_three = 1.0 / (n_total * added(rho3, nc))
@@ -443,7 +444,7 @@
             pltpu.VMEM((nk, L), f32),
             pltpu.VMEM((nc, nk, L), f32),
             pltpu.VMEM((nc, nk, L), bf16),
-            pltpu.VMEM((nc, nk, L), f32),
+            pltpu.VMEM((nc, nk, L), bf16),
             pltpu.VMEM((nd, nj, L), f32),
             pltpu.VMEM((nd, nj, L), f32),
             pltpu.VMEM((nd, nj, L), f32),

time: 64.8 us -> 64.6 us (level)
  no operation moved by 1% of the time
where the time goes in v5:
time: 64.6 us
  Pallas kernels  63.9 us (99%)
    pallas_call x1, Pallas kernels, on_device(): pl.pallas_call(functools.partial(kernel, nd, nc, side, float(rows * nd),...  62.9 us

profile of v5, /device:TPU:1, one launch (start us, length us, event | category | flops | bytes accessed | tf_op | source)
XLA Modules:
  0.0 64.6 jit_solution(9018117283365368365)
XLA Ops:
  0.6 62.9 %sinkhorn.1 = (bf16[512,1024]{1,0:T(8,128)(2,1)S(1)}, f32[16,128]{1,0:T(8,128)S(1)}, f32[4,128]{1,0:T(4,128)S(1)}) custom-call(f32[4,128]{1,0:T(4,128)} %bitcast.4, bf16[512,1024]{1,0:T(8,128)(2,1)} %c_hbm.1, bf16[2048,1024]{1,0:T(8,128)(2,1)} %e_hbm.1), custom_call_target="tpu_custom_call" | custom-call | flops 4294967296 | bytes 6291456 | tf_op jit(solution)/shard_map/sinkhorn/pallas_call | solution.py:423
  63.5 1.0 %closing.1 = (bf16[512,1024]{1,0:T(8,128)(2,1)}, f32[16,128]{1,0:T(8,128)}, f32[4,128]{1,0:T(4,128)}) custom-call(bf16[512,1024]{1,0:T(8,128)(2,1)S(1)} %get-tuple-element.9.c_in, f32[16,128]{1,0:T(8,128)S(1)} %get-tuple-element.10.r_in, f32[4,128]{1,0:T(4,128)S(1)} %get-tuple-element.11.k_in), custom_call_target="tpu_custom_call" | custom-call | tf_op jit(solution)/shard_map/closing/pallas_call | solution.py:477

commit v6 on v4

--- a/solution.py
+++ b/solution.py
@@ -38,6 +38,14 @@
         half = x.shape[0] // 2
         x = act(x[:half], x[half:])
     return x
+
+
+def over_rows(part, rows, act):
+    folded = [fold(part(pl.ds(start, SUB)), act) for start in range(0, rows, SUB)]
+    total = folded[0]
+    for piece in folded[1:]:
+        total = act(total, piece)
+    return total
 
 
 def kernel(
@@ -108,8 +116,8 @@
             tm[b * (BLK // L) + h] = product[:, h * L : (h + 1) * L]
         for h in range(BLK // L):
             k = b * (BLK // L) + h
-            peak = jnp.max(fold(tm[k] + gcol[...], jnp.maximum), axis=0, keepdims=True)
-            mass = jnp.sum(fold(jnp.exp2(tm[k] + gcol[...] - peak), jnp.add), axis=0, keepdims=True)
+            peak = jnp.max(over_rows(lambda r: tm[k, r, :] + gcol[r, :], kc, jnp.maximum), axis=0, keepdims=True)
+            mass = jnp.sum(over_rows(lambda r: jnp.exp2(tm[k, r, :] + gcol[r, :] - peak), kc, jnp.add), axis=0, keepdims=True)
             l_all[ce, pl.ds(k, 1), :] = peak + jnp.log2(mass)
         return carry
 
@@ -223,9 +231,12 @@
         col1[pl.ds(t * L, L), :] = to_column(lift[t : t + 1, :])
 
     def second_rows(k, carry):
-        value = am[k] * col1[...]
-        am[k] = value
-        rsum[pl.ds(k, 1), :] = jnp.sum(fold(value, jnp.add), axis=0, keepdims=True)
+        def lifted(r):
+            value = am[k, r, :] * col1[r, :]
+            am[k, r, :] = value
+            return value
+
+        rsum[pl.ds(k, 1), :] = jnp.sum(over_rows(lifted, kc, jnp.add), axis=0, keepdims=True)
         return carry
 
     lax.fori_loop(0, nk, second_rows, 0, unroll=2)
@@ -258,7 +269,7 @@
         col1[pl.ds(t * L, L), :] = to_column(v_two[t : t + 1, :])
 
     def third_rows(k, carry):
-        rho3[ce, pl.ds(k, 1), :] = jnp.sum(fold(am[k] * col1[...], jnp.add), axis=0, keepdims=True)
+        rho3[ce, pl.ds(k, 1), :] = jnp.sum(over_rows(lambda r: am[k, r, :] * col1[r, :], kc, jnp.add), axis=0, keepdims=True)
         return carry
 
     lax.fori_loop(0, nk, third_rows, 0, unroll=2)

time: 64.8 us -> 64.7 us (level)
  no operation moved by 1% of the time
where the time goes in v6:
time: 64.7 us; the launch traced here: 64.6 us
  Pallas kernels  64 us (99%)
    pallas_call x1, Pallas kernels, on_device(): pl.pallas_call(functools.partial(kernel, nd, nc, side, float(rows * nd),...  63 us

profile of v6, /device:TPU:1, one launch (start us, length us, event | category | flops | bytes accessed | tf_op | source)
XLA Modules:
  0.0 64.6 jit_solution(4058417654425793457)
XLA Ops:
  0.6 63.0 %sinkhorn.1 = (bf16[512,1024]{1,0:T(8,128)(2,1)S(1)}, f32[16,128]{1,0:T(8,128)S(1)}, f32[4,128]{1,0:T(4,128)S(1)}) custom-call(f32[4,128]{1,0:T(4,128)} %bitcast.4, bf16[512,1024]{1,0:T(8,128)(2,1)} %c_hbm.1, bf16[2048,1024]{1,0:T(8,128)(2,1)} %e_hbm.1), custom_call_target="tpu_custom_call" | custom-call | flops 4294967296 | bytes 6291456 | tf_op jit(solution)/shard_map/sinkhorn/pallas_call | solution.py:433
  63.6 1.0 %closing.1 = (bf16[512,1024]{1,0:T(8,128)(2,1)}, f32[16,128]{1,0:T(8,128)}, f32[4,128]{1,0:T(4,128)}) custom-call(bf16[512,1024]{1,0:T(8,128)(2,1)S(1)} %get-tuple-element.9.c_in, f32[16,128]{1,0:T(8,128)S(1)} %get-tuple-element.10.r_in, f32[4,128]{1,0:T(4,128)S(1)} %get-tuple-element.11.k_in), custom_call_target="tpu_custom_call" | custom-call | tf_op jit(solution)/shard_map/closing/pallas_call | solution.py:487
